TPU v7x, 32 devices: a whole 2x2x4 slice. The times are simulated.
32 devices in a mesh: runs: 2 (over x), tm: 8 (over z, y), hyd: 2 (over core).
Axes of the slice: x: 2, y: 2, z: 4, core: 2. Of those that a mesh axis runs over, the one named last changes fastest.
Arguments:
- record: bfloat16 [524160, 1024], P(('runs', 'tm'), 'hyd'), parts along dimension 0, may hold values from -6 to 6
- chips: int32 [4095], replicated, may hold values from -1 to 1, as said below
- steer_lags: int32 [1024, 256], P('hyd'), may hold values from 0 to 7
Outputs:
- power: float32 [128, 512, 256], P('runs', 'tm', 'hyd'), parts along dimension 0
There are 2 independent parts, one for each index of `runs`. A program takes and returns all parts, laid end to end along the dimension named above; an argument that names none is the same for every part. Nothing has to cross between parts.
Inputs may be any that keep to these rules, and one draw needn't show every extreme that they name: The chips are +1 or -1 and form one period of a maximal-length sequence of period 4095, starting at a drawn phase.
All inputs are finite; a program needn't handle non-finite values.
Results may differ from a plain program's by a relative error of at most 0.0047.
Values may be sent and summed in bfloat16 or wider, within the bound.
A program may use at most 256 MiB of HBM per device.

v0:
```python
import math
import jax
import jax.numpy as jnp
from jax import lax
from jax.sharding import PartitionSpec as P

CODE = 4095
HYDRO = 1024
DELAYS = 512
PERIODS = 64
BEAMS = 256
MAXLAG = 8


def passed_along(array, axis, by):
    length = lax.axis_size(axis)
    pairs = [(i, i + by) for i in range(length) if 0 <= i + by < length]
    return lax.ppermute(array, axis, pairs)


def toeplitz_code(chips):
    seg_len = CODE + DELAYS - 1
    padded = jnp.concatenate([chips.astype(jnp.float32), jnp.zeros((DELAYS,), jnp.float32)])
    tiled = jnp.tile(padded, DELAYS)[: DELAYS * seg_len]
    return tiled.reshape(DELAYS, seg_len).astype(jnp.bfloat16)


def dft_table(length):
    freq = jnp.arange(length, dtype=jnp.int32)
    phase = (freq[:, None] * freq[None, :] % length).astype(jnp.float32) * (2.0 * math.pi / length)
    weight = 1.0 / math.sqrt(length)
    return jnp.concatenate([jnp.cos(phase) * weight, -jnp.sin(phase) * weight], 0).astype(
        jnp.bfloat16
    )


def body(record, chips, steer_lags):
    hyd_local = record.shape[1]
    tm_size = lax.axis_size("tm")
    local_periods = PERIODS // tm_size
    delay_rows = DELAYS // tm_size
    seg_len = CODE + DELAYS - 1
    norm_code = 1.0 / math.sqrt(CODE)
    tail_rows = passed_along(record[: DELAYS - 1], "tm", -1)
    extended = jnp.concatenate([record, tail_rows], 0)
    toeplitz = toeplitz_code(chips)
    profile_list = []
    for period in range(local_periods):
        segment = extended[period * CODE : period * CODE + seg_len]
        profile_list.append(
            (jnp.dot(toeplitz, segment, preferred_element_type=jnp.float32) * norm_code).astype(
                jnp.bfloat16
            )
        )
    profiles = jnp.stack(profile_list, 0)
    transform = dft_table(PERIODS)
    received = lax.all_to_all(profiles, "tm", split_axis=1, concat_axis=0, tiled=True)
    trailing = received.shape[1:]
    flattened = received.reshape(received.shape[0], -1)
    spectral = jnp.dot(transform, flattened, preferred_element_type=jnp.float32).astype(
        jnp.bfloat16
    )
    spectrum = spectral.reshape((2, received.shape[0]) + trailing)
    next_rows = passed_along(spectrum[:, :, : MAXLAG - 1, :], "tm", -1)
    spec_ext = jnp.concatenate([spectrum, next_rows], 2)
    norm_hydro = 1.0 / math.sqrt(HYDRO)
    shifted_list = [
        spec_ext[:, :, offset : offset + delay_rows, :].reshape(2 * PERIODS * delay_rows, hyd_local)
        for offset in range(MAXLAG)
    ]
    beam_local = BEAMS // lax.axis_size("hyd")
    partial_sum = jnp.zeros((2 * PERIODS * delay_rows, BEAMS), jnp.float32)
    for offset in range(MAXLAG):
        selector = (steer_lags == offset).astype(jnp.bfloat16)
        partial_sum = partial_sum + jnp.dot(
            shifted_list[offset], selector, preferred_element_type=jnp.float32
        )
    summed = lax.psum(partial_sum * norm_hydro, "hyd")
    owned = lax.dynamic_slice_in_dim(summed, lax.axis_index("hyd") * beam_local, beam_local, 1)
    owned = owned.reshape(2, PERIODS, delay_rows, beam_local)
    return owned[0] * owned[0] + owned[1] * owned[1]


def solution(mesh):
    in_specs = (P(("runs", "tm"), "hyd"), P(), P("hyd", None))
    out_specs = P("runs", "tm", "hyd")
    return jax.shard_map(body, mesh=mesh, in_specs=in_specs, out_specs=out_specs, check_vma=False)
```

profile of v0, /device:TPU:0, one launch (start us, length us, event | category | flops | bytes accessed | tf_op | source)
XLA Modules:
  0.0 408.6 jit_solution(9783359401931948476)
XLA Ops:
  6.5 1.1 slice.73
  7.6 1.3 collective-permute-start
  8.9 0.7 convert_element_type.49
  9.6 2.5 tile.10
  12.1 11.8 %tile.11 = bf16[2358784]{0:T(1024)(128)(2,1)} reshape(bf16[512,4607]{1,0:T(8,128)(2,1)} %tile.10) | data formatting | bytes 9435136 | tf_op jit(solution)/shard_map/tile | solution.py:24
  23.9 5.7 %slice.85 = bf16[2358272]{0:T(1024)(128)(2,1)} slice(bf16[2358784]{0:T(1024)(128)(2,1)} %tile.11), slice={[0:2358272]} | slice | bytes 9433088 | tf_op jit(solution)/shard_map/slice | solution.py:24
  29.6 11.3 %convert_element_type.50 = bf16[512,4606]{1,0:T(8,128)(2,1)} reshape(bf16[2358272]{0:T(1024)(128)(2,1)} %slice.85) | data formatting | bytes 9433088 | tf_op jit(solution)/shard_map/convert_element_type | solution.py:25
  40.9 7.3 %fusion.65 = bf16[8,512,512]{2,1,0:T(8,128)(2,1)} fusion(bf16[512,4606]{1,0:T(8,128)(2,1)} %convert_element_type.50, bf16[32760,512]{1,0:T(8,128)(2,1)} %param.3), kind=kOutput, calls=%fused_computation.47 | convolution fusion | flops 2415394816 | bytes 9961472 | tf_op jit(solution)/shard_map/dot_general | solution.py:51
  48.3 0.0 slice-start.5
  48.3 5.9 %fusion.73 = bf16[8,512,512]{2,1,0:T(8,128)(2,1)} fusion(bf16[8,512,512]{2,1,0:T(8,128)(2,1)} %fusion.65, bf16[512,4606]{1,0:T(8,128)(2,1)S(1)} %copy-done.1, bf16[32760,512]{1,0:T(8,128)(2,1)} %param.3), kind=kOutput, calls=%fused_computation.51 | convolution fusion | flops 2415394816 | bytes 9959424 | tf_op jit(solution)/shard_map/dot_general | solution.py:51
  54.2 6.6 %fusion.79 = bf16[8,512,512]{2,1,0:T(8,128)(2,1)} fusion(bf16[8,512,512]{2,1,0:T(8,128)(2,1)} %fusion.73, bf16[512,4606]{1,0:T(8,128)(2,1)S(1)} %copy-done.1, bf16[32760,512]{1,0:T(8,128)(2,1)} %param.3), kind=kOutput, calls=%fused_computation.53 | convolution fusion | flops 2415394816 | bytes 9959424 | tf_op jit(solution)/shard_map/dot_general | solution.py:51
  60.9 0.0 slice-done.8
  60.9 1.4 slice-done.9
  62.3 3.7 fusion.85
  66.0 3.5 fusion.91
  69.5 3.5 fusion.97
  73.0 3.5 fusion.103
  76.5 0.0 collective-permute-done
  76.5 5.9 %fusion.69 = bf16[8,512,512]{2,1,0:T(8,128)(2,1)} fusion(bf16[8,512,512]{2,1,0:T(8,128)(2,1)} %fusion.103, bf16[512,4606]{1,0:T(8,128)(2,1)} %convert_element_type.50, bf16[511,512]{1,0:T(8,128)(2,1)S(1)} %collective-permute-done, bf16[32760,512]{1,0:T(8,128)(2,1)S(1)} %bitcast.82), kind=kOutput, calls=%fused_computation.49 | convolution fusion | flops 2424827904 | bytes 39312384 | tf_op jit(solution)/shard_map/dot_general | solution.py:51
  82.5 6.9 %copy.5 = bf16[8,512,512]{2,0,1:T(8,128)(2,1)} copy(bf16[8,512,512]{2,1,0:T(8,128)(2,1)} %fusion.69) | data formatting | bytes 8388608 | tf_op jit(solution)/shard_map/stack | solution.py:55
  89.3 8.4 %all-to-all-start = ((bf16[8,512,512]{2,0,1:T(8,128)(2,1)}), bf16[8,512,512]{2,0,1:T(8,128)(2,1)}, u32[]{:S(2)}, u32[]{:S(2)}) async-start(bf16[8,512,512]{2,0,1:T(8,128)(2,1)} %copy.5), calls=%async_computation | async-start | bytes 8388608 | tf_op jit(solution)/shard_map/all_to_all | solution.py:57
  97.8 0.0 all-reduce.3.cloned.1.call-start
  97.8 0.2 multiply_convert_fusion
  98.0 92.8 %all-to-all-done = bf16[8,512,512]{2,0,1:T(8,128)(2,1)} async-done(((bf16[8,512,512]{2,0,1:T(8,128)(2,1)}), bf16[8,512,512]{2,0,1:T(8,128)(2,1)}, u32[]{:S(2)}, u32[]{:S(2)}) %all-to-all-start) | async-done | bytes 4194336 | tf_op jit(solution)/shard_map/all_to_all | solution.py:57
  190.8 3.8 copy.14
  194.6 2.6 copy.10
  197.1 5.6 %convolution_convert_fusion = bf16[128,32768]{1,0:T(8,128)(2,1)} fusion(bf16[64,32768]{1,0:T(8,128)(2,1)S(1)} %bitcast.83, bf16[64,64]{1,0:T(8,128)(2,1)S(1)} %get-tuple-element.12, bf16[64,64]{1,0:T(8,128)(2,1)S(1)} %get-tuple-element.13), kind=kOutput, calls=%fused_computation | convolution fusion | flops 541097984 | bytes 12599296 | tf_op jit(solution)/shard_map/dot_general | solution.py:60
  202.7 13.6 %reshape_reshape.3 = bf16[8192,512]{1,0:T(8,128)(2,1)} reshape(bf16[128,32768]{1,0:T(8,128)(2,1)} %convolution_convert_fusion) | data formatting | bytes 16777216 | tf_op jit(solution)/shard_map/reshape;reshape | solution.py:68
  216.3 10.2 %copy.11 = bf16[16,8,64,512]{3,2,1,0:T(8,128)(2,1)} copy(bf16[16,8,64,512]{3,1,2,0:T(8,128)(2,1)} %bitcast.69) | data formatting | bytes 16777216
  226.6 8.0 %constant_dynamic-update-slice_fusion = bf16[2,64,71,512]{3,2,1,0:T(8,128)(2,1)} fusion(bf16[2,64,64,512]{3,2,1,0:T(8,128)(2,1)} %bitcast.79), kind=kLoop, calls=%fused_computation.94 | loop fusion | bytes 16777216
  234.6 1.3 slice.86
  235.9 0.3 copy.9
  236.2 1.3 collective-permute-start.1
  237.5 9.1 %fusion.113 = f32[8192,256]{1,0:T(8,128)} fusion(bf16[8192,512]{1,0:T(8,128)(2,1)} %reshape_reshape.3, s32[512,256]{1,0:T(8,128)S(1)} %copy-done), kind=kOutput, calls=%fused_computation.70 | convolution fusion | flops 2147614720 | bytes 17301504 | tf_op jit(solution)/shard_map/dot_general | solution.py:75
  246.7 12.5 %collective-permute-done.1 = bf16[2,64,7,512]{3,1,2,0:T(8,128)(2,1)S(1)} collective-permute-done((bf16[2,64,7,512]{3,1,2,0:T(8,128)(2,1)S(1)}, bf16[2,64,7,512]{3,1,2,0:T(8,128)(2,1)S(1)}, u32[]{:S(2)}, u32[]{:S(2)}) %collective-permute-start.1) | collective-permute-done | bytes 917536 | tf_op jit(solution)/shard_map/ppermute | solution.py:18
  259.1 1.6 copy_dynamic-update-slice_fusion
  260.7 52.8 %fusion.142 = (bf16[2,64,64,512]{3,2,1,0:T(8,128)(2,1)}, bf16[2,64,64,512]{3,2,1,0:T(8,128)(2,1)}, bf16[2,64,64,512]{3,2,1,0:T(8,128)(2,1)}, bf16[2,64,64,512]{3...) fusion(bf16[2,64,71,512]{3,2,1,0:T(8,128)(2,1)} %copy_dynamic-u, ...), kind=kLoop, calls=%fused_computation.106 | loop fusion | bytes 117440512 | tf_op jit(solution)/shard_map/slice | solution.py:68
  313.6 8.4 %convolution_add_fusion.6 = f32[8192,256]{1,0:T(8,128)S(1)} fusion(f32[8192,256]{1,0:T(8,128)} %fusion.113, bf16[8192,512]{1,0:T(8,128)(2,1)} %bitcast.78, s32[512,256]{1,0:T(8,128)S(1)} %copy-done), kind=kOutput, calls=%fused_computation.8 | convolution fusion | flops 2149711872 | bytes 25690112 | tf_op jit(solution)/shard_map/dot_general | solution.py:75
  322.0 0.0 slice-start
  322.0 6.1 %convolution_add_fusion.5 = f32[8192,256]{1,0:T(8,128)S(1)} fusion(f32[8192,256]{1,0:T(8,128)S(1)} %convolution_add_fusion.6, bf16[8192,512]{1,0:T(8,128)(2,1)} %bitcast.77, s32[512,256]{1,0:T(8,128)S(1)} %copy-done), kind=kOutput, calls=%fused_computation.7 | convolution fusion | flops 2149711872 | bytes 25690112 | tf_op jit(solution)/shard_map/dot_general | solution.py:75
  328.1 6.1 %convolution_add_fusion.4 = f32[8192,256]{1,0:T(8,128)S(1)} fusion(f32[8192,256]{1,0:T(8,128)S(1)} %convolution_add_fusion.5, bf16[8192,512]{1,0:T(8,128)(2,1)} %bitcast.76, s32[512,256]{1,0:T(8,128)S(1)} %copy-done), kind=kOutput, calls=%fused_computation.6 | convolution fusion | flops 2149711872 | bytes 25690112 | tf_op jit(solution)/shard_map/dot_general | solution.py:75
  334.3 2.4 convolution_add_fusion.3
  336.7 6.3 %convolution_add_fusion.2 = f32[8192,256]{1,0:T(8,128)S(1)} fusion(f32[8192,256]{1,0:T(8,128)S(1)} %convolution_add_fusion.3, bf16[8192,512]{1,0:T(8,128)(2,1)} %bitcast.72, s32[512,256]{1,0:T(8,128)S(1)} %copy-done), kind=kOutput, calls=%fused_computation.4 | convolution fusion | flops 2149711872 | bytes 25690112 | tf_op jit(solution)/shard_map/dot_general | solution.py:75
  343.0 6.0 %convolution_add_fusion.1 = f32[8192,256]{1,0:T(8,128)S(1)} fusion(f32[8192,256]{1,0:T(8,128)S(1)} %convolution_add_fusion.2, bf16[8192,512]{1,0:T(8,128)(2,1)} %bitcast.71, s32[512,256]{1,0:T(8,128)S(1)} %copy-done), kind=kOutput, calls=%fused_computation.3 | convolution fusion | flops 2149711872 | bytes 25690112 | tf_op jit(solution)/shard_map/dot_general | solution.py:75
  349.0 9.2 %fusion = f32[8192,256]{1,0:T(8,128)} fusion(f32[8192,256]{1,0:T(8,128)S(1)} %convolution_add_fusion.1, bf16[8192,512]{1,0:T(8,128)(2,1)} %bitcast.70, s32[512,256]{1,0:T(8,128)S(1)} %copy-done), kind=kOutput, calls=%fused_computation.2 | convolution fusion | flops 2151809024 | bytes 25690112 | tf_op jit(solution)/shard_map/dot_general | solution.py:75
  358.2 0.0 all-reduce.3.cloned.1.call-update
  358.2 39.2 %all-reduce.3.cloned.1.call-done = f32[8192,256]{1,0:T(8,128)} async-done(((f32[8192,256]{1,0:T(8,128)}), f32[8192,256]{1,0:T(8,128)}) %all-reduce.3.cloned.1.call-update) | async-done | bytes 8388624 | tf_op jit(solution)/shard_map/psum | solution.py:78
  397.5 3.8 fusion.17
  (23 shorter events, 0.0 us)
Async XLA Ops:
  7.6 68.9 %collective-permute-start = (bf16[511,512]{1,0:T(8,128)(2,1)S(1)}, bf16[511,512]{1,0:T(8,128)(2,1)S(1)}, u32[]{:S(2)}, u32[]{:S(2)}) collective-permute-start(bf16[511,512]{1,0:T(8,128)(2,1)S(1)} %slice.73), channel_id=1, source_target_pairs={{2,0},{4,2},{6,4},{8,6},{10,8},{12,10},{14,12},{3,1},{5,3},{7,5},{... | collective-permute-start | bytes 1569800 | tf_op jit(solution)/shard_map/ppermute | solution.py:18
  40.9 7.3 %copy-start.1 = (bf16[512,4606]{1,0:T(8,128)(2,1)S(1)}, bf16[512,4606]{1,0:T(8,128)(2,1)}, u32[]{:S(2)}) copy-start(bf16[512,4606]{1,0:T(8,128)(2,1)} %convert_element_type.50) | copy-start | bytes 14149636
  48.2 12.6 %slice-start.2 = ((s8[33546240]{0:T(1024)(128)(4,1)}), s8[4194304]{0:T(1024)(128)(4,1)S(1)}, s32[]{:S(2)}) async-start(s8[33546240]{0:T(1024)(128)(4,1)} %bitcast.81), calls=%async_computation.4 | async-start | bytes 8388608
  48.2 12.6 %slice-start.3 = ((s8[33546240]{0:T(1024)(128)(4,1)}), s8[4194304]{0:T(1024)(128)(4,1)S(1)}, s32[]{:S(2)}) async-start(s8[33546240]{0:T(1024)(128)(4,1)} %bitcast.81), calls=%async_computation.5 | async-start | bytes 8388608
  48.2 12.6 %slice-start.4 = ((s8[33546240]{0:T(1024)(128)(4,1)}), s8[4194304]{0:T(1024)(128)(4,1)S(1)}, s32[]{:S(2)}) async-start(s8[33546240]{0:T(1024)(128)(4,1)} %bitcast.81), calls=%async_computation.6 | async-start | bytes 8388608
  48.3 12.6 %slice-start.5 = ((s8[33546240]{0:T(1024)(128)(4,1)}), s8[4194304]{0:T(1024)(128)(4,1)S(1)}, s32[]{:S(2)}) async-start(s8[33546240]{0:T(1024)(128)(4,1)} %bitcast.81), calls=%async_computation.7 | async-start | bytes 8388608
  48.3 12.6 %slice-start.6 = ((s8[33546240]{0:T(1024)(128)(4,1)}), s8[4194304]{0:T(1024)(128)(4,1)S(1)}, s32[]{:S(2)}) async-start(s8[33546240]{0:T(1024)(128)(4,1)} %bitcast.81), calls=%async_computation.8 | async-start | bytes 8388608
  54.2 6.6 %slice-start.7 = ((s8[33546240]{0:T(1024)(128)(4,1)}), s8[4194304]{0:T(1024)(128)(4,1)S(1)}, s32[]{:S(2)}) async-start(s8[33546240]{0:T(1024)(128)(4,1)} %bitcast.81), calls=%async_computation.9 | async-start | bytes 8388608
  54.2 6.7 %slice-start.8 = ((s8[33546240]{0:T(1024)(128)(4,1)}), s8[4194304]{0:T(1024)(128)(4,1)S(1)}, s32[]{:S(2)}) async-start(s8[33546240]{0:T(1024)(128)(4,1)} %bitcast.81), calls=%async_computation.10 | async-start | bytes 8388608
  54.2 8.0 %slice-start.9 = ((s8[33546240]{0:T(1024)(128)(4,1)}), s8[4186112]{0:T(1024)(128)(4,1)S(1)}, s32[]{:S(2)}) async-start(s8[33546240]{0:T(1024)(128)(4,1)} %bitcast.81), calls=%async_computation.11 | async-start | bytes 8372224
  89.3 101.4 %all-to-all-start = ((bf16[8,512,512]{2,0,1:T(8,128)(2,1)}), bf16[8,512,512]{2,0,1:T(8,128)(2,1)}, u32[]{:S(2)}, u32[]{:S(2)}) async-start(bf16[8,512,512]{2,0,1:T(8,128)(2,1)} %copy.5), calls=%async_computation | async-start | bytes 8388608 | tf_op jit(solution)/shard_map/all_to_all | solution.py:57
  97.8 299.7 %all-reduce.3.cloned.1.call-start = ((), (), s32[]{:S(2)}) async-start(), calls=%async_computation.1 | async-start | bytes 16777216 | tf_op jit(solution)/shard_map/psum | solution.py:78
  226.6 10.9 %copy-start = (s32[512,256]{1,0:T(8,128)S(1)}, s32[512,256]{1,0:T(8,128)}, u32[]{:S(2)}) copy-start(s32[512,256]{1,0:T(8,128)} %param.5) | copy-start | bytes 1572868
  236.2 22.9 %collective-permute-start.1 = (bf16[2,64,7,512]{3,1,2,0:T(8,128)(2,1)S(1)}, bf16[2,64,7,512]{3,1,2,0:T(8,128)(2,1)S(1)}, u32[]{:S(2)}, u32[]{:S(2)}) collective-permute-start(bf16[2,64,7,512]{3,1,2,0:T(8,128)(2,1)S(1)} %copy.9), channel_id=1, source_target_pairs={{2,0},{4,2},{6,4},{8,6},{10,8},{12,10},{14,12},{3,1},{5,3},{7,5},{... | collective-permute-start | bytes 2752520 | tf_op jit(solution)/shard_map/ppermute | solution.py:18
  322.0 12.3 %slice-start = ((s8[8388608]{0:T(1024)(128)(4,1)}), s8[4194304]{0:T(1024)(128)(4,1)S(1)}, s32[]{:S(2)}) async-start(s8[8388608]{0:T(1024)(128)(4,1)} %bitcast.73), calls=%async_computation.2 | async-start | bytes 8388608
  328.1 6.2 %slice-start.1 = ((s8[8388608]{0:T(1024)(128)(4,1)}), s8[4194304]{0:T(1024)(128)(4,1)S(1)}, s32[]{:S(2)}) async-start(s8[8388608]{0:T(1024)(128)(4,1)} %bitcast.73), calls=%async_computation.3 | async-start | bytes 8388608
Sparse Core Ops, SparseCore 0:
  358.3 39.0 all-reduce.2
where the time goes:
time: 416 us; the launch traced here: 409 us
  waiting for transfers between devices  145 us (35%)
  local copies, waits for them, and re-layouts  135 us (32%)
  matrix products  99.3 us (24%)
  between operations  14.1 us (3%)
  starting transfers between devices  11 us (3%)
  other arithmetic  4.64 us (1%)
    all_to_all x1, waiting for transfers between devices, body(): lax.all_to_all(profiles, 'tm', split_axis=1, concat_axis=0, tiled=True)  92.8 us
    dot_general x8, matrix products, body(): jnp.dot(shifted_list[offset], selector, preferred_element_type=jnp.float32)  53.7 us
    slice x1, local copies, waits for them, and re-layouts, body(): spec_ext[:, :, offset:offset + delay_rows, :]  52.8 us
    dot_general x8, matrix products, body(): jnp.dot(toeplitz, segment, preferred_element_type=jnp.float32) * norm_code  40 us
    psum x1, waiting for transfers between devices, body(): summed = lax.psum(partial_sum * norm_hydro, 'hyd')  39.2 us
    unnamed x28, local copies, waits for them, and re-layouts  22.6 us
    another operation x2, local copies, waits for them, and re-layouts, toeplitz_code(): tiled = jnp.tile(padded, DELAYS)[:DELAYS * seg_len]  14.3 us
    another operation x1, local copies, waits for them, and re-layouts, body(): spec_ext[:, :, offset:offset + delay_rows, :]  13.6 us
  transfers between devices with their start and end apart: 4, of which 3 were waited for; matrix products, arithmetic and copies ran while one was open for 18% of the time, Pallas kernels for 0%

commit v1 on v0

--- a/solution.py
+++ b/solution.py
@@ -75,7 +75,7 @@
         partial_sum = partial_sum + jnp.dot(
             shifted_list[offset], selector, preferred_element_type=jnp.float32
         )
-    summed = lax.psum(partial_sum * norm_hydro, "hyd")
+    summed = lax.all_gather(partial_sum * norm_hydro, axis_name="hyd").sum(axis=0)
     owned = lax.dynamic_slice_in_dim(summed, lax.axis_index("hyd") * beam_local, beam_local, 1)
     owned = owned.reshape(2, PERIODS, delay_rows, beam_local)
     return owned[0] * owned[0] + owned[1] * owned[1]

time: 416 us -> 418 us (level)
  other arithmetic: 4.64 us -> 15.9 us
  waiting for transfers between devices: 145 us -> 136 us
    psum x1 -> x0, waiting for transfers between devices: 39.2 us -> none  [body(): summed = lax.psum(partial_sum * norm_hydro, 'hyd')]
    all_gather x0 -> x1, waiting for transfers between devices: none -> 30.4 us  [body(): lax.all_gather(partial_sum * norm_hydro, axis_name='hyd').sum(axis=0)]
    reduce_sum x0 -> x1, other arithmetic: none -> 11.3 us  [body(): lax.all_gather(partial_sum * norm_hydro, axis_name='hyd').sum(axis=0)]
where the time goes in v1:
time: 418 us; the launch traced here: 411 us
  waiting for transfers between devices  136 us (33%)
  local copies, waits for them, and re-layouts  135 us (32%)
  matrix products  99.3 us (24%)
  other arithmetic  15.9 us (4%)
  between operations  14.1 us (3%)
  starting transfers between devices  11 us (3%)
    all_to_all x1, waiting for transfers between devices, body(): lax.all_to_all(profiles, 'tm', split_axis=1, concat_axis=0, tiled=True)  92.8 us
    dot_general x8, matrix products, body(): jnp.dot(shifted_list[offset], selector, preferred_element_type=jnp.float32)  53.6 us
    slice x1, local copies, waits for them, and re-layouts, body(): spec_ext[:, :, offset:offset + delay_rows, :]  52.8 us
    dot_general x8, matrix products, body(): jnp.dot(toeplitz, segment, preferred_element_type=jnp.float32) * norm_code  40 us
    all_gather x1, waiting for transfers between devices, body(): lax.all_gather(partial_sum * norm_hydro, axis_name='hyd').sum(axis=0)  30.4 us
    unnamed x28, local copies, waits for them, and re-layouts  22.6 us
    another operation x2, local copies, waits for them, and re-layouts, toeplitz_code(): tiled = jnp.tile(padded, DELAYS)[:DELAYS * seg_len]  14.3 us
    another operation x1, local copies, waits for them, and re-layouts, body(): spec_ext[:, :, offset:offset + delay_rows, :]  13.6 us
  transfers between devices with their start and end apart: 4, of which 3 were waited for; matrix products, arithmetic and copies ran while one was open for 18% of the time, Pallas kernels for 0%

profile of v1, /device:TPU:0, one launch (start us, length us, event | category | flops | bytes accessed | tf_op | source)
XLA Modules:
  0.0 411.1 jit_solution(8085662283641363496)
XLA Ops:
  6.5 1.1 slice.73
  7.6 1.3 collective-permute-start
  8.9 0.7 convert_element_type.49
  9.6 2.5 tile.10
  12.1 11.8 %tile.11 = bf16[2358784]{0:T(1024)(128)(2,1)} reshape(bf16[512,4607]{1,0:T(8,128)(2,1)} %tile.10) | data formatting | bytes 9435136 | tf_op jit(solution)/shard_map/tile | solution.py:24
  23.9 5.7 %slice.85 = bf16[2358272]{0:T(1024)(128)(2,1)} slice(bf16[2358784]{0:T(1024)(128)(2,1)} %tile.11), slice={[0:2358272]} | slice | bytes 9433088 | tf_op jit(solution)/shard_map/slice | solution.py:24
  29.6 11.3 %convert_element_type.50 = bf16[512,4606]{1,0:T(8,128)(2,1)} reshape(bf16[2358272]{0:T(1024)(128)(2,1)} %slice.85) | data formatting | bytes 9433088 | tf_op jit(solution)/shard_map/convert_element_type | solution.py:25
  40.9 7.3 %fusion.65 = bf16[8,512,512]{2,1,0:T(8,128)(2,1)} fusion(bf16[512,4606]{1,0:T(8,128)(2,1)} %convert_element_type.50, bf16[32760,512]{1,0:T(8,128)(2,1)} %param.3), kind=kOutput, calls=%fused_computation.47 | convolution fusion | flops 2415394816 | bytes 9961472 | tf_op jit(solution)/shard_map/dot_general | solution.py:51
  48.3 0.0 slice-start.5
  48.3 5.9 %fusion.73 = bf16[8,512,512]{2,1,0:T(8,128)(2,1)} fusion(bf16[8,512,512]{2,1,0:T(8,128)(2,1)} %fusion.65, bf16[512,4606]{1,0:T(8,128)(2,1)S(1)} %copy-done.1, bf16[32760,512]{1,0:T(8,128)(2,1)} %param.3), kind=kOutput, calls=%fused_computation.51 | convolution fusion | flops 2415394816 | bytes 9959424 | tf_op jit(solution)/shard_map/dot_general | solution.py:51
  54.2 6.6 %fusion.79 = bf16[8,512,512]{2,1,0:T(8,128)(2,1)} fusion(bf16[8,512,512]{2,1,0:T(8,128)(2,1)} %fusion.73, bf16[512,4606]{1,0:T(8,128)(2,1)S(1)} %copy-done.1, bf16[32760,512]{1,0:T(8,128)(2,1)} %param.3), kind=kOutput, calls=%fused_computation.53 | convolution fusion | flops 2415394816 | bytes 9959424 | tf_op jit(solution)/shard_map/dot_general | solution.py:51
  60.9 0.0 slice-done.8
  60.9 1.4 slice-done.9
  62.3 3.7 fusion.85
  66.0 3.5 fusion.91
  69.5 3.5 fusion.97
  73.0 3.5 fusion.103
  76.5 0.0 collective-permute-done
  76.5 5.9 %fusion.69 = bf16[8,512,512]{2,1,0:T(8,128)(2,1)} fusion(bf16[8,512,512]{2,1,0:T(8,128)(2,1)} %fusion.103, bf16[512,4606]{1,0:T(8,128)(2,1)} %convert_element_type.50, bf16[511,512]{1,0:T(8,128)(2,1)S(1)} %collective-permute-done, bf16[32760,512]{1,0:T(8,128)(2,1)S(1)} %bitcast.83), kind=kOutput, calls=%fused_computation.49 | convolution fusion | flops 2424827904 | bytes 39312384 | tf_op jit(solution)/shard_map/dot_general | solution.py:51
  82.5 6.9 %copy.5 = bf16[8,512,512]{2,0,1:T(8,128)(2,1)} copy(bf16[8,512,512]{2,1,0:T(8,128)(2,1)} %fusion.69) | data formatting | bytes 8388608 | tf_op jit(solution)/shard_map/stack | solution.py:55
  89.3 8.4 %all-to-all-start = ((bf16[8,512,512]{2,0,1:T(8,128)(2,1)}), bf16[8,512,512]{2,0,1:T(8,128)(2,1)}, u32[]{:S(2)}, u32[]{:S(2)}) async-start(bf16[8,512,512]{2,0,1:T(8,128)(2,1)} %copy.5), calls=%async_computation | async-start | bytes 8388608 | tf_op jit(solution)/shard_map/all_to_all | solution.py:57
  97.8 0.0 all-gather.3.cloned.1.call-start
  97.8 0.2 multiply_convert_fusion
  98.0 92.8 %all-to-all-done = bf16[8,512,512]{2,0,1:T(8,128)(2,1)} async-done(((bf16[8,512,512]{2,0,1:T(8,128)(2,1)}), bf16[8,512,512]{2,0,1:T(8,128)(2,1)}, u32[]{:S(2)}, u32[]{:S(2)}) %all-to-all-start) | async-done | bytes 4194336 | tf_op jit(solution)/shard_map/all_to_all | solution.py:57
  190.8 3.8 copy.14
  194.6 2.6 copy.10
  197.1 5.6 %convolution_convert_fusion = bf16[128,32768]{1,0:T(8,128)(2,1)} fusion(bf16[64,32768]{1,0:T(8,128)(2,1)S(1)} %bitcast.84, bf16[64,64]{1,0:T(8,128)(2,1)S(1)} %get-tuple-element.12, bf16[64,64]{1,0:T(8,128)(2,1)S(1)} %get-tuple-element.13), kind=kOutput, calls=%fused_computation | convolution fusion | flops 541097984 | bytes 12599296 | tf_op jit(solution)/shard_map/dot_general | solution.py:60
  202.7 13.6 %reshape_reshape.3 = bf16[8192,512]{1,0:T(8,128)(2,1)} reshape(bf16[128,32768]{1,0:T(8,128)(2,1)} %convolution_convert_fusion) | data formatting | bytes 16777216 | tf_op jit(solution)/shard_map/reshape;reshape | solution.py:68
  216.3 10.2 %copy.11 = bf16[16,8,64,512]{3,2,1,0:T(8,128)(2,1)} copy(bf16[16,8,64,512]{3,1,2,0:T(8,128)(2,1)} %bitcast.70) | data formatting | bytes 16777216
  226.6 8.0 %constant_dynamic-update-slice_fusion = bf16[2,64,71,512]{3,2,1,0:T(8,128)(2,1)} fusion(bf16[2,64,64,512]{3,2,1,0:T(8,128)(2,1)} %bitcast.80), kind=kLoop, calls=%fused_computation.94 | loop fusion | bytes 16777216
  234.6 1.3 slice.86
  235.9 0.3 copy.9
  236.2 1.3 collective-permute-start.1
  237.5 9.1 %fusion.113 = f32[8192,256]{1,0:T(8,128)} fusion(bf16[8192,512]{1,0:T(8,128)(2,1)} %reshape_reshape.3, s32[512,256]{1,0:T(8,128)S(1)} %copy-done), kind=kOutput, calls=%fused_computation.70 | convolution fusion | flops 2147614720 | bytes 17301504 | tf_op jit(solution)/shard_map/dot_general | solution.py:75
  246.7 12.5 %collective-permute-done.1 = bf16[2,64,7,512]{3,1,2,0:T(8,128)(2,1)S(1)} collective-permute-done((bf16[2,64,7,512]{3,1,2,0:T(8,128)(2,1)S(1)}, bf16[2,64,7,512]{3,1,2,0:T(8,128)(2,1)S(1)}, u32[]{:S(2)}, u32[]{:S(2)}) %collective-permute-start.1) | collective-permute-done | bytes 917536 | tf_op jit(solution)/shard_map/ppermute | solution.py:18
  259.1 1.6 copy_dynamic-update-slice_fusion
  260.7 52.8 %fusion.142 = (bf16[2,64,64,512]{3,2,1,0:T(8,128)(2,1)}, bf16[2,64,64,512]{3,2,1,0:T(8,128)(2,1)}, bf16[2,64,64,512]{3,2,1,0:T(8,128)(2,1)}, bf16[2,64,64,512]{3...) fusion(bf16[2,64,71,512]{3,2,1,0:T(8,128)(2,1)} %copy_dynamic-u, ...), kind=kLoop, calls=%fused_computation.106 | loop fusion | bytes 117440512 | tf_op jit(solution)/shard_map/slice | solution.py:68
  313.6 8.4 %convolution_add_fusion.6 = f32[8192,256]{1,0:T(8,128)S(1)} fusion(f32[8192,256]{1,0:T(8,128)} %fusion.113, bf16[8192,512]{1,0:T(8,128)(2,1)} %bitcast.79, s32[512,256]{1,0:T(8,128)S(1)} %copy-done), kind=kOutput, calls=%fused_computation.8 | convolution fusion | flops 2149711872 | bytes 25690112 | tf_op jit(solution)/shard_map/dot_general | solution.py:75
  322.0 6.1 %convolution_add_fusion.5 = f32[8192,256]{1,0:T(8,128)S(1)} fusion(f32[8192,256]{1,0:T(8,128)S(1)} %convolution_add_fusion.6, bf16[8192,512]{1,0:T(8,128)(2,1)} %bitcast.78, s32[512,256]{1,0:T(8,128)S(1)} %copy-done), kind=kOutput, calls=%fused_computation.7 | convolution fusion | flops 2149711872 | bytes 25690112 | tf_op jit(solution)/shard_map/dot_general | solution.py:75
  328.1 6.1 %convolution_add_fusion.4 = f32[8192,256]{1,0:T(8,128)S(1)} fusion(f32[8192,256]{1,0:T(8,128)S(1)} %convolution_add_fusion.5, bf16[8192,512]{1,0:T(8,128)(2,1)} %bitcast.77, s32[512,256]{1,0:T(8,128)S(1)} %copy-done), kind=kOutput, calls=%fused_computation.6 | convolution fusion | flops 2149711872 | bytes 25690112 | tf_op jit(solution)/shard_map/dot_general | solution.py:75
  334.3 2.4 convolution_add_fusion.3
  336.7 6.3 %convolution_add_fusion.2 = f32[8192,256]{1,0:T(8,128)S(1)} fusion(f32[8192,256]{1,0:T(8,128)S(1)} %convolution_add_fusion.3, bf16[8192,512]{1,0:T(8,128)(2,1)} %bitcast.73, s32[512,256]{1,0:T(8,128)S(1)} %copy-done), kind=kOutput, calls=%fused_computation.4 | convolution fusion | flops 2149711872 | bytes 25690112 | tf_op jit(solution)/shard_map/dot_general | solution.py:75
  343.0 6.0 %convolution_add_fusion.1 = f32[8192,256]{1,0:T(8,128)S(1)} fusion(f32[8192,256]{1,0:T(8,128)S(1)} %convolution_add_fusion.2, bf16[8192,512]{1,0:T(8,128)(2,1)} %bitcast.72, s32[512,256]{1,0:T(8,128)S(1)} %copy-done), kind=kOutput, calls=%fused_computation.3 | convolution fusion | flops 2149711872 | bytes 25690112 | tf_op jit(solution)/shard_map/dot_general | solution.py:75
  349.0 9.1 %fusion = f32[8192,256]{1,0:T(8,128)} fusion(f32[8192,256]{1,0:T(8,128)S(1)} %convolution_add_fusion.1, bf16[8192,512]{1,0:T(8,128)(2,1)} %bitcast.71, s32[512,256]{1,0:T(8,128)S(1)} %copy-done), kind=kOutput, calls=%fused_computation.2 | convolution fusion | flops 2151809024 | bytes 25690112 | tf_op jit(solution)/shard_map/dot_general | solution.py:75
  358.2 0.0 all-gather.3.cloned.1.call-update
  358.2 30.4 %all-gather.3.cloned.1.call-done = f32[16384,256]{1,0:T(8,128)} async-done(((f32[8192,256]{1,0:T(8,128)}), f32[16384,256]{1,0:T(8,128)}) %all-gather.3.cloned.1.call-update) | async-done | bytes 16777232 | tf_op jit(solution)/shard_map/all_gather | solution.py:78
  388.6 11.3 %reduce_sum.9 = f32[8192,256]{1,0:T(8,128)} reduce(f32[2,8192,256]{2,1,0:T(8,128)} %bitcast.85, f32[]{:T(128)} %constant.9.clone.1), dimensions={0}, to_apply=%region_0.1 | reduce | flops 2097152 | bytes 25165828 | tf_op jit(solution)/shard_map/reduce_sum | solution.py:78
  399.9 3.8 fusion.17
  (24 shorter events, 0.1 us)
Async XLA Ops:
  7.6 68.9 %collective-permute-start = (bf16[511,512]{1,0:T(8,128)(2,1)S(1)}, bf16[511,512]{1,0:T(8,128)(2,1)S(1)}, u32[]{:S(2)}, u32[]{:S(2)}) collective-permute-start(bf16[511,512]{1,0:T(8,128)(2,1)S(1)} %slice.73), channel_id=1, source_target_pairs={{2,0},{4,2},{6,4},{8,6},{10,8},{12,10},{14,12},{3,1},{5,3},{7,5},{... | collective-permute-start | bytes 1569800 | tf_op jit(solution)/shard_map/ppermute | solution.py:18
  40.9 7.3 %copy-start.1 = (bf16[512,4606]{1,0:T(8,128)(2,1)S(1)}, bf16[512,4606]{1,0:T(8,128)(2,1)}, u32[]{:S(2)}) copy-start(bf16[512,4606]{1,0:T(8,128)(2,1)} %convert_element_type.50) | copy-start | bytes 14149636
  48.2 12.6 %slice-start.2 = ((s8[33546240]{0:T(1024)(128)(4,1)}), s8[4194304]{0:T(1024)(128)(4,1)S(1)}, s32[]{:S(2)}) async-start(s8[33546240]{0:T(1024)(128)(4,1)} %bitcast.82), calls=%async_computation.4 | async-start | bytes 8388608
  48.2 12.6 %slice-start.3 = ((s8[33546240]{0:T(1024)(128)(4,1)}), s8[4194304]{0:T(1024)(128)(4,1)S(1)}, s32[]{:S(2)}) async-start(s8[33546240]{0:T(1024)(128)(4,1)} %bitcast.82), calls=%async_computation.5 | async-start | bytes 8388608
  48.2 12.6 %slice-start.4 = ((s8[33546240]{0:T(1024)(128)(4,1)}), s8[4194304]{0:T(1024)(128)(4,1)S(1)}, s32[]{:S(2)}) async-start(s8[33546240]{0:T(1024)(128)(4,1)} %bitcast.82), calls=%async_computation.6 | async-start | bytes 8388608
  48.3 12.6 %slice-start.5 = ((s8[33546240]{0:T(1024)(128)(4,1)}), s8[4194304]{0:T(1024)(128)(4,1)S(1)}, s32[]{:S(2)}) async-start(s8[33546240]{0:T(1024)(128)(4,1)} %bitcast.82), calls=%async_computation.7 | async-start | bytes 8388608
  48.3 12.6 %slice-start.6 = ((s8[33546240]{0:T(1024)(128)(4,1)}), s8[4194304]{0:T(1024)(128)(4,1)S(1)}, s32[]{:S(2)}) async-start(s8[33546240]{0:T(1024)(128)(4,1)} %bitcast.82), calls=%async_computation.8 | async-start | bytes 8388608
  54.2 6.6 %slice-start.7 = ((s8[33546240]{0:T(1024)(128)(4,1)}), s8[4194304]{0:T(1024)(128)(4,1)S(1)}, s32[]{:S(2)}) async-start(s8[33546240]{0:T(1024)(128)(4,1)} %bitcast.82), calls=%async_computation.9 | async-start | bytes 8388608
  54.2 6.7 %slice-start.8 = ((s8[33546240]{0:T(1024)(128)(4,1)}), s8[4194304]{0:T(1024)(128)(4,1)S(1)}, s32[]{:S(2)}) async-start(s8[33546240]{0:T(1024)(128)(4,1)} %bitcast.82), calls=%async_computation.10 | async-start | bytes 8388608
  54.2 8.0 %slice-start.9 = ((s8[33546240]{0:T(1024)(128)(4,1)}), s8[4186112]{0:T(1024)(128)(4,1)S(1)}, s32[]{:S(2)}) async-start(s8[33546240]{0:T(1024)(128)(4,1)} %bitcast.82), calls=%async_computation.11 | async-start | bytes 8372224
  89.3 101.4 %all-to-all-start = ((bf16[8,512,512]{2,0,1:T(8,128)(2,1)}), bf16[8,512,512]{2,0,1:T(8,128)(2,1)}, u32[]{:S(2)}, u32[]{:S(2)}) async-start(bf16[8,512,512]{2,0,1:T(8,128)(2,1)} %copy.5), calls=%async_computation | async-start | bytes 8388608 | tf_op jit(solution)/shard_map/all_to_all | solution.py:57
  97.8 290.9 %all-gather.3.cloned.1.call-start = ((), (), s32[]{:S(2)}) async-start(), calls=%async_computation.1 | async-start | bytes 25165824 | tf_op jit(solution)/shard_map/all_gather | solution.py:78
  226.6 10.9 %copy-start = (s32[512,256]{1,0:T(8,128)S(1)}, s32[512,256]{1,0:T(8,128)}, u32[]{:S(2)}) copy-start(s32[512,256]{1,0:T(8,128)} %param.5) | copy-start | bytes 1572868
  236.2 22.9 %collective-permute-start.1 = (bf16[2,64,7,512]{3,1,2,0:T(8,128)(2,1)S(1)}, bf16[2,64,7,512]{3,1,2,0:T(8,128)(2,1)S(1)}, u32[]{:S(2)}, u32[]{:S(2)}) collective-permute-start(bf16[2,64,7,512]{3,1,2,0:T(8,128)(2,1)S(1)} %copy.9), channel_id=1, source_target_pairs={{2,0},{4,2},{6,4},{8,6},{10,8},{12,10},{14,12},{3,1},{5,3},{7,5},{... | collective-permute-start | bytes 2752520 | tf_op jit(solution)/shard_map/ppermute | solution.py:18
  322.0 12.3 %slice-start = ((s8[8388608]{0:T(1024)(128)(4,1)}), s8[4194304]{0:T(1024)(128)(4,1)S(1)}, s32[]{:S(2)}) async-start(s8[8388608]{0:T(1024)(128)(4,1)} %bitcast.74), calls=%async_computation.2 | async-start | bytes 8388608
  328.1 6.2 %slice-start.1 = ((s8[8388608]{0:T(1024)(128)(4,1)}), s8[4194304]{0:T(1024)(128)(4,1)S(1)}, s32[]{:S(2)}) async-start(s8[8388608]{0:T(1024)(128)(4,1)} %bitcast.74), calls=%async_computation.3 | async-start | bytes 8388608
Sparse Core Ops, SparseCore 0:
  358.3 30.2 all-gather.2
